TPU v7x, 256 devices: a whole 4x4x8 slice. The times are simulated.
256 devices in a mesh: gx: 32 (over z, x_lo, core), gy: 8 (over x_hi, y).
Axes of the slice: x: 4 (x_hi: 2, x_lo: 2; x = x_hi * 2 + x_lo), y: 4, z: 8, core: 2. Of those that a mesh axis runs over, the one named last changes fastest.
Arguments:
- field: bfloat16 [64, 64, 8, 384], P('gx', 'gy'), may hold values from -54 to 54
- cotangent: bfloat16 [64, 64, 8, 384], P('gx', 'gy'), may hold values from -6 to 6
- win_qkv: bfloat16 [384, 1152], replicated, may hold values from -2 to 2
- win_out: bfloat16 [384, 384], replicated, may hold values from -0.3125 to 0.3125
- axial_qkv: bfloat16 [384, 1152], replicated, may hold values from -2 to 2
- axial_out: bfloat16 [384, 384], replicated, may hold values from -0.3125 to 0.3125
- mlp_in: bfloat16 [384, 1536], replicated, may hold values from -0.3125 to 0.3125
- mlp_out: bfloat16 [1536, 384], replicated, may hold values from -0.15625 to 0.15625
- pattern: int32 [6, 3], replicated, may hold values from 0 to 7, as said below
Outputs:
- layer_output: bfloat16 [64, 64, 8, 384], P('gx', 'gy')
- field_grad: float32 [64, 64, 8, 384], P('gx', 'gy')
Inputs may be any that keep to these rules, and one draw needn't show every extreme that they name: `pattern`: row h holds (base + dilation * j) mod 8 for j = 0 to 2, with a base per head and a dilation of 1 to 3 per head.
All inputs are finite; a program needn't handle non-finite values.
Results may differ from a plain program's by a relative error of at most 0.02.
The roundings to bfloat16 on the way count: a program that leaves them out, or rounds other values in their place, can miss the bound.
Values may be sent and summed in bfloat16 or wider, within the bound.
A program may use at most 128 MiB of HBM per device.

v0:
```python
import functools

import jax
import jax.numpy as jnp
from jax import lax
from jax.experimental import pallas as pl
from jax.experimental.pallas import tpu as pltpu
from jax.sharding import PartitionSpec as P

F32 = jnp.float32
BF16 = jnp.bfloat16
C = 384
FF = 1536
PAIRS = 3
TOK = 128
KEYS = 576
EPSILON = 1e-06
MASKED = -1e30
MESH = pl.DeviceIdType.MESH

SIDES = [(1, 1), (-1, -1), (1, -1), (-1, 1), (0, 1), (0, -1), (1, 0), (-1, 0)]
PEERS = [3, 5, 2, 6, 4, 1, 7]


def nn(a, b):
    return lax.dot_general(a, b, (((1,), (0,)), ((), ())), preferred_element_type=F32)


def nt(a, b):
    return lax.dot_general(a, b, (((1,), (1,)), ((), ())), preferred_element_type=F32)


def inverse_rms(v):
    return lax.rsqrt(jnp.sum(v * v, axis=-1, keepdims=True) * (1.0 / C) + EPSILON)


def norm_back(v, r, upstream):
    inner = jnp.sum(v * upstream, axis=-1, keepdims=True) * (1.0 / C)
    return r * upstream - v * (r * r * r * inner)


def iota(shape, dim):
    return lax.broadcasted_iota(jnp.int32, shape, dim)


def stacked(pair):
    first = iota(pair.shape, 1) < 64
    upper = jnp.where(first, pair, 0.0)
    return jnp.concatenate([upper, pair - upper], axis=0).astype(BF16)


def diagonal(both):
    return jnp.concatenate([both[:64, :128], both[64:, 128:]], axis=0)


def softmax_keys(scores):
    e = jnp.exp(scores - jnp.max(scores, axis=0, keepdims=True))
    return e * (1.0 / jnp.sum(e, axis=0, keepdims=True))


def lanes(p, base=0):
    return slice(base + 128 * p, base + 128 * (p + 1))


def kernel(
    nx,
    ny,
    field,
    cot,
    win_qkv_h,
    win_out_h,
    axial_qkv_h,
    axial_out_h,
    mlp_in_h,
    mlp_out_h,
    pattern_h,
    out_ref,
    grad_ref,
    win_qkv,
    win_out,
    axial_qkv,
    axial_out,
    mlp_in,
    mlp_out,
    pattern,
    rim,
    cot_own,
    cot_send,
    cot_recv,
    s1_send,
    s1_recv,
    lo_send,
    lo_recv,
    g1_send,
    g1_recv,
    dn_send,
    rim_big,
    rim_small,
    weights1,
    kv1,
    kt1,
    bias1,
    q1,
    local_sem,
    halo_send,
    halo_recv,
    a2a_send,
    a2a_recv,
    push_send,
    push_recv,
):
    gx = lax.axis_index("gx")
    gy = lax.axis_index("gy")

    def step(index, by, size):
        moved = index + by
        if by > 0:
            return jnp.where(moved >= size, moved - size, moved)
        return jnp.where(moved < 0, moved + size, moved) if by else index

    def at(dx, dy):
        return (step(gx, dx, nx), step(gy, dy, ny))

    barrier = pltpu.get_barrier_semaphore()
    greeted = SIDES + [(0, d) for d in range(2, ny - 1)]
    for dx, dy in greeted:
        pl.semaphore_signal(barrier, inc=1, device_id=at(dx, dy), device_id_type=MESH)

    local = []
    for index, (src, dst) in enumerate(
        [
            (field, rim.at[2:4, 1:5]),
            (cot, cot_own),
            (win_qkv_h, win_qkv),
            (win_out_h, win_out),
            (axial_qkv_h, axial_qkv),
            (axial_out_h, axial_out),
            (mlp_in_h, mlp_in),
            (mlp_out_h, mlp_out),
            (pattern_h, pattern),
        ]
    ):
        copy = pltpu.make_async_copy(src, dst, local_sem.at[index])
        copy.start()
        local.append(copy)
    local[0].wait()
    pl.semaphore_wait(barrier, len(greeted))

    own_y = {0: slice(1, 5), 1: slice(4, 5), -1: slice(1, 2)}
    land_x = {1: slice(0, 2), 0: slice(2, 4), -1: slice(4, 6)}
    land_y = {1: slice(0, 1), 0: slice(1, 5), -1: slice(5, 6)}
    halo = []
    for index, (dx, dy) in enumerate(SIDES):
        copy = pltpu.make_async_remote_copy(
            src_ref=rim.at[2:4, own_y[dy]],
            dst_ref=rim.at[land_x[dx], land_y[dy]],
            send_sem=halo_send.at[index],
            recv_sem=halo_recv.at[index],
            device_id=at(dx, dy),
            device_id_type=MESH,
        )
        copy.start()
        halo.append(copy)

    def exchange(send, recv, group):
        copies = []
        for d in PEERS:
            peer = step(gy, d, ny)
            copy = pltpu.make_async_remote_copy(
                src_ref=send.at[peer],
                dst_ref=recv.at[gy],
                send_sem=a2a_send.at[group, d],
                recv_sem=a2a_recv.at[group, d],
                device_id=(gx, peer),
                device_id_type=MESH,
            )
            copy.start()
            copies.append(copy)
        recv[pl.ds(gy, 1)] = send[pl.ds(gy, 1)]
        return copies

    def arrived(send, recv, group):
        for d in PEERS:
            source = step(gy, -d, ny)
            pltpu.make_async_remote_copy(
                src_ref=send.at[source],
                dst_ref=recv.at[source],
                send_sem=a2a_send.at[group, d],
                recv_sem=a2a_recv.at[group, d],
                device_id=(gx, source),
                device_id_type=MESH,
            ).wait_recv()
        return recv[...].reshape(TOK, C)

    row, col = iota((TOK, TOK), 0), iota((TOK, TOK), 1)
    to_zxy = jnp.where(row == (col & 7) * 16 + (col >> 3), 1.0, 0.0).astype(BF16)
    to_xyz = jnp.where(col == (row & 7) * 16 + (row >> 3), 1.0, 0.0).astype(BF16)
    eye = jnp.where(row == col, 1.0, 0.0).astype(BF16)

    local[1].wait()
    cot_send[...] = nn(to_zxy, cot_own[...].reshape(TOK, C)).astype(BF16).reshape(8, 16, C)
    cot_copies = exchange(cot_send, cot_recv, 0)

    key, query = iota((96, TOK), 0), iota((96, TOK), 1)
    gap_y = (key >> 3) - 2 - (query & 7)
    gap_z = ((key & 7) - (query >> 4) + 2) & 7
    near = (jnp.abs(gap_y) <= 2) & (gap_z <= 4)
    second = (query >> 3) & 1
    plane_bias = jnp.where(near, 0.0, MASKED)
    for plane in range(6):
        block = plane_bias
        if plane == 0:
            block = jnp.where(second == 0, plane_bias, MASKED)
        if plane == 5:
            block = jnp.where(second == 1, plane_bias, MASKED)
        bias1[96 * plane : 96 * (plane + 1), :] = block

    field_own = rim[2:4, 1:5].reshape(TOK, C)
    field_f = field_own.astype(F32)
    r1 = inverse_rms(field_f)
    normed1_zxy = nn(to_zxy, (field_f * r1).astype(BF16)).astype(BF16)
    field_zxy = nn(to_zxy, field_own)
    local[2].wait()
    query1 = nn(normed1_zxy, win_qkv[:, 0:C]).astype(BF16).astype(F32) * 0.125
    for p in range(PAIRS):
        q1[p] = stacked(query1[:, lanes(p)])
    for copy in halo:
        copy.wait_recv()
    all_f = rim[...].reshape(KEYS, C).astype(F32)
    normed_all = (all_f * inverse_rms(all_f)).astype(BF16)
    kv1[...] = nn(normed_all, win_qkv[:, C : 3 * C]).astype(BF16)
    bias_both = jnp.concatenate([bias1[...], bias1[...]], axis=1)
    attended = []
    for p in range(PAIRS):
        weights = softmax_keys(nt(kv1[:, lanes(p)], q1[p]) + bias_both).astype(BF16)
        weights1[p] = weights
        vt = nt(eye, kv1[:, lanes(p, C)]).astype(BF16)
        attended.append(nt(eye, diagonal(nn(vt, weights)).astype(BF16)))
    attended = jnp.concatenate(attended, axis=1).astype(BF16)
    local[3].wait()
    s1_send[...] = (field_zxy + nn(attended, win_out[...])).astype(BF16).reshape(8, 16, C)
    s1_copies = exchange(s1_send, s1_recv, 1)

    for p in range(PAIRS):
        kt1[p] = nt(eye, kv1[:, lanes(p)]).astype(BF16)
    for copy in local[4:]:
        copy.wait()
    off = ((row >> 4) - (col >> 4)) & 7
    same_line = ((row ^ col) & 8) == 0
    bias2 = []
    for head in range(2 * PAIRS):
        hit = off == 0
        for j in range(3):
            hit = hit | (off == pattern[j, head])
        bias2.append(jnp.where(hit & same_line, 0.0, MASKED))

    gradient_bf = arrived(cot_send, cot_recv, 0)
    gradient = gradient_bf.astype(F32)
    d_hidden = [
        nt(gradient_bf, mlp_out[512 * c : 512 * (c + 1), :]) for c in range(FF // 512)
    ]
    stream1 = arrived(s1_send, s1_recv, 1).astype(F32)
    r2 = inverse_rms(stream1)
    triple2 = nn((stream1 * r2).astype(BF16), axial_qkv[...]).astype(BF16)
    query2 = triple2[:, 0:C].astype(F32) * 0.125
    q2 = [stacked(query2[:, lanes(p)]) for p in range(PAIRS)]
    weights2 = []
    attended2 = []
    for p in range(PAIRS):
        pair_bias = jnp.concatenate([bias2[2 * p], bias2[2 * p + 1]], axis=1)
        weights = softmax_keys(nt(triple2[:, lanes(p, C)], q2[p]) + pair_bias).astype(BF16)
        weights2.append(weights)
        vt = nt(eye, triple2[:, lanes(p, 2 * C)]).astype(BF16)
        attended2.append(nt(eye, diagonal(nn(vt, weights)).astype(BF16)))
    attended2 = jnp.concatenate(attended2, axis=1).astype(BF16)
    stream2 = (stream1 + nn(attended2, axial_out[...])).astype(BF16).astype(F32)

    r3 = inverse_rms(stream2)
    normed3 = (stream2 * r3).astype(BF16)
    hidden = []
    back = None
    for c in range(FF // 512):
        part = slice(512 * c, 512 * (c + 1))
        a = nn(normed3, mlp_in[:, part])
        square = a * a
        t = jnp.tanh(0.7978845608028654 * (a + 0.044715 * (a * square)))
        half = 0.5 * (1.0 + t)
        hidden.append((a * half).astype(BF16))
        slope = half + (0.5 * a) * (1.0 - t * t) * (
            0.7978845608028654 + (3 * 0.044715 * 0.7978845608028654) * square
        )
        term = nt((d_hidden[c] * slope).astype(BF16), mlp_in[:, part])
        back = term if back is None else back + term
    grad2 = gradient + norm_back(stream2, r3, back)

    back2 = nt(grad2.astype(BF16), axial_out[...])
    d_query, d_key, d_value = [], [], []
    for p in range(PAIRS):
        upstream = stacked(back2[:, lanes(p)])
        d_weights = nt(triple2[:, lanes(p, 2 * C)], upstream)
        weights = weights2[p].astype(F32)
        product = weights * d_weights
        delta = jnp.sum(product, axis=0, keepdims=True)
        d_scores = (product - weights * delta).astype(BF16)
        kt = nt(eye, triple2[:, lanes(p, C)]).astype(BF16)
        dqt = (diagonal(nn(kt, d_scores)) * 0.125).astype(BF16)
        d_query.append(nt(eye, dqt))
        d_key.append(nn(d_scores, q2[p]))
        d_value.append(nn(weights2[p], upstream))
    d_triple2 = jnp.concatenate(d_query + d_key + d_value, axis=1).astype(BF16)
    grad1 = grad2 + norm_back(stream1, r2, nt(d_triple2, axial_qkv[...]))
    g1_send[...] = grad1.astype(BF16).reshape(8, 16, C)
    g1_copies = exchange(g1_send, g1_recv, 3)

    hidden_out = nn(jnp.concatenate(hidden, axis=1), mlp_out[...])
    lo_send[...] = (stream2 + hidden_out).astype(BF16).reshape(8, 16, C)
    lo_copies = exchange(lo_send, lo_recv, 2)

    grad1_bf = arrived(g1_send, g1_recv, 3)
    back1 = nt(grad1_bf, win_out[...])
    scores_back, d_key, d_value = [], [], []
    for p in range(PAIRS):
        upstream = stacked(back1[:, lanes(p)])
        d_weights = nt(kv1[:, lanes(p, C)], upstream)
        weights = weights1[p].astype(F32)
        product = weights * d_weights
        delta = jnp.sum(product, axis=0, keepdims=True)
        d_scores = (product - weights * delta).astype(BF16)
        scores_back.append(d_scores)
        d_key.append(nn(d_scores, q1[p]).astype(BF16))
        d_value.append(nn(weights1[p], upstream).astype(BF16))
    d_kv = jnp.concatenate(d_key + d_value, axis=1)
    back_x = {-1: slice(0, 2), 0: slice(2, 4), 1: slice(4, 6)}
    back_y = {-1: slice(0, 1), 0: slice(1, 5), 1: slice(5, 6)}
    push = []
    for side in (1, -1, 0):
        rows = slice(192 * (side + 1), 192 * (side + 2))
        dn_block = nt(d_kv[rows], win_qkv[:, C : 3 * C]).reshape(2, 6, 16, C)
        dn_send[back_x[side]] = dn_block.astype(BF16)
        for index, (dx, dy) in enumerate(SIDES):
            if dx != side:
                continue
            dst = rim_big.at[index - 6] if dy == 0 else rim_small.at[index]
            copy = pltpu.make_async_remote_copy(
                src_ref=dn_send.at[back_x[dx], back_y[dy]],
                dst_ref=dst,
                send_sem=push_send.at[index],
                recv_sem=push_recv.at[index],
                device_id=at(dx, dy),
                device_id_type=MESH,
            )
            copy.start()
            push.append(copy)

    d_query = [
        (diagonal(nn(kt1[p], scores_back[p])) * 0.125).astype(BF16) for p in range(PAIRS)
    ]
    d_query = nt(to_xyz, jnp.concatenate(d_query, axis=0)).astype(BF16)
    d_normed = dn_block[:, 1:5].reshape(TOK, C) + nt(d_query, win_qkv[:, 0:C])
    grad1_xyz = nn(to_xyz, grad1_bf)
    out_ref[...] = nn(to_xyz, arrived(lo_send, lo_recv, 2)).astype(BF16)
    for copy in push:
        copy.wait_recv()
    d_normed = d_normed + (rim_big[0].astype(F32) + rim_big[1].astype(F32)).reshape(TOK, C)
    below = [i for i, (_, dy) in enumerate(SIDES) if dy == 1]
    above = [i for i, (_, dy) in enumerate(SIDES) if dy == -1]
    first = sum(rim_small[i].astype(F32) for i in below).reshape(2, 16, C)
    last = sum(rim_small[i].astype(F32) for i in above).reshape(2, 16, C)
    none = jnp.zeros((32, C), F32)
    edges = jnp.concatenate([first[0], none, last[0], first[1], none, last[1]], axis=0)
    field_f = rim[2:4, 1:5].reshape(TOK, C).astype(F32)
    grad_ref[...] = grad1_xyz + norm_back(field_f, inverse_rms(field_f), d_normed + edges)

    for copy in halo + cot_copies + s1_copies + lo_copies + g1_copies + push:
        copy.wait_send()


def shards(nx, ny, field, cotangent, *rest):
    block = (2, 4, 16, C)
    tiles = (8, 16, C)
    vmem = pltpu.VMEM
    dma = pltpu.SemaphoreType.DMA
    weights, pattern = rest[:6], rest[6]
    in_hbm = pl.BlockSpec(memory_space=pltpu.HBM)
    in_vmem = pl.BlockSpec(memory_space=pltpu.VMEM)
    layer_output, field_grad = pl.pallas_call(
        functools.partial(kernel, nx, ny),
        out_shape=(
            jax.ShapeDtypeStruct((TOK, C), BF16),
            jax.ShapeDtypeStruct((TOK, C), F32),
        ),
        in_specs=[in_hbm] * 9,
        out_specs=(in_vmem, in_vmem),
        scratch_shapes=[vmem(w.shape, BF16) for w in weights]
        + [pltpu.SMEM((3, 6), jnp.int32), vmem((6, 6, 16, C), BF16)]
        + [vmem(tiles, BF16)] * 9
        + [
            vmem((6, 6, 16, C), BF16),
            vmem((2,) + block, BF16),
            vmem((6, 2, 1, 16, C), BF16),
            vmem((PAIRS, KEYS, 256), BF16),
            vmem((KEYS, 2 * C), BF16),
            vmem((PAIRS, TOK, KEYS), BF16),
            vmem((KEYS, TOK), F32),
            vmem((PAIRS, 256, TOK), BF16),
            dma((9,)),
            dma((8,)),
            dma((8,)),
            dma((4, 8)),
            dma((4, 8)),
            dma((8,)),
            dma((8,)),
        ],
        compiler_params=pltpu.CompilerParams(
            collective_id=0, has_side_effects=True, vmem_limit_bytes=60 * 1024 * 1024
        ),
    )(field.reshape(block), cotangent.reshape(tiles), *weights, pattern.T)
    return layer_output.reshape(field.shape), field_grad.reshape(field.shape)


def solution(mesh):
    split = P("gx", "gy", None, None)
    return jax.shard_map(
        functools.partial(shards, mesh.shape["gx"], mesh.shape["gy"]),
        mesh=mesh,
        in_specs=(split, split) + (P(),) * 7,
        out_specs=(split, split),
        check_vma=False,
    )
```

profile of v0, /device:TPU:1, one launch (start us, length us, event | category | flops | bytes accessed | tf_op | source)
XLA Modules:
  0.0 45.7 jit_solution(7089640559255797748)
XLA Ops:
  0.6 41.9 %shard_map.104 = (bf16[128,384]{1,0:T(8,128)(2,1)}, f32[128,384]{1,0:T(8,128)}) custom-call(bf16[2,4,16,384]{3,2,1,0:T(8,128)(2,1)} %bitcast.7, bf16[8,16,384]{2,1,0:T(8,128)(2,1)} %bitcast.8, bf16[384,1152]{1,0:T(8,128)(2,1)} %win_qkv_h.1, bf16[384,384]{1,0:T(8,128)(2,1)} %win_out_h.1, bf16[384,1152]{1,0:T(8,128)(2,1)} %axial_qkv_h.1, ...), custom_call_target="tpu_custom_call" | custom-call | tf_op jit(solution)/shard_map/pallas_call | solution.py:386
  42.5 1.5 %copy.13 = bf16[2,8,8,384]{3,2,1,0:T(8,128)(2,1)} copy(bf16[2,8,8,384]{3,2,1,0:T(8,128)(2,1)} %bitcast.6) | data formatting | bytes 196608
  44.0 1.6 %copy.14 = f32[2,8,8,384]{3,2,1,0:T(8,128)} copy(f32[2,8,8,384]{3,2,1,0:T(8,128)} %bitcast.5) | data formatting | bytes 393216
where the time goes:
time: 45.8 us; the launch traced here: 45.7 us
  Pallas kernels  41.9 us (91%)
  local copies, waits for them, and re-layouts  3.16 us (7%)
  between operations  0.64 us (1%)
    pallas_call x1, Pallas kernels, shards(): pl.pallas_call(functools.partial(kernel, nx, ny), out_shape=(jax.ShapeDty...  41.9 us
    unnamed x2, local copies, waits for them, and re-layouts  3.16 us

commit v1 on v0

v1 whole, which is shorter than its diff:
```python
import functools

import jax
import jax.numpy as jnp
from jax import lax
from jax.experimental import pallas as pl
from jax.experimental.pallas import tpu as pltpu
from jax.sharding import PartitionSpec as P

F32 = jnp.float32
BF16 = jnp.bfloat16
C = 384
FF = 1536
PAIRS = 3
TOK = 128
KEYS = 576
OWN, AROUND, EARLY, EDGES = slice(0, 128), slice(128, 384), slice(0, 384), slice(384, 576)
EPSILON = 1e-06
MASKED = -1e30
MESH = pl.DeviceIdType.MESH

SIDES = [(1, 1), (-1, -1), (1, -1), (-1, 1), (0, 1), (0, -1), (1, 0), (-1, 0)]
PEERS = [2, 6, 1, 3, 5, 7, 0, 4]


def nn(a, b):
    return lax.dot_general(a, b, (((1,), (0,)), ((), ())), preferred_element_type=F32)


def nt(a, b):
    return lax.dot_general(a, b, (((1,), (1,)), ((), ())), preferred_element_type=F32)


def inverse_rms(v):
    return lax.rsqrt(jnp.sum(v * v, axis=-1, keepdims=True) * (1.0 / C) + EPSILON)


def norm_back(v, r, upstream):
    inner = jnp.sum(v * upstream, axis=-1, keepdims=True) * (1.0 / C)
    return r * upstream - v * (r * r * r * inner)


def iota(shape, dim):
    return lax.broadcasted_iota(jnp.int32, shape, dim)


def stacked(pair):
    first = iota(pair.shape, 1) < 64
    upper = jnp.where(first, pair, 0.0)
    return jnp.concatenate([upper, pair - upper], axis=0).astype(BF16)


def diagonal(both):
    return jnp.concatenate([both[:64, :128], both[64:, 128:]], axis=0)


def abreast(both):
    return jnp.concatenate([both[:TOK], both[TOK:]], axis=1)


def lanes(p, base=0):
    return slice(base + 128 * p, base + 128 * (p + 1))


def kernel(
    nx,
    ny,
    field,
    cot,
    win_qkv_h,
    win_out_h,
    axial_qkv_h,
    axial_out_h,
    mlp_in_h,
    mlp_out_h,
    pattern_h,
    out_ref,
    grad_ref,
    win_qkv,
    win_out,
    axial_qkv,
    axial_out,
    mlp_in,
    mlp_out,
    pattern,
    own,
    sides,
    edges,
    cot_own,
    cot_send,
    cot_recv,
    s1_send,
    s1_recv,
    lo_send,
    lo_recv,
    g1_send,
    g1_recv,
    dn_send,
    dn_recv,
    weights1,
    kv1,
    kt1,
    vt1,
    ot1,
    scores1,
    bias1,
    q1,
    local_sem,
    halo_send,
    halo_recv,
    a2a_send,
    a2a_recv,
    push_send,
    push_recv,
):
    gx = lax.axis_index("gx")
    gy = lax.axis_index("gy")

    partner = gx + 2 - 4 * ((gx >> 1) & 1)

    def step(index, by, size):
        moved = index + by
        if by > 0:
            return jnp.where(moved >= size, moved - size, moved)
        return jnp.where(moved < 0, moved + size, moved) if by else index

    def at(dx, dy):
        return (step(gx, dx, nx), step(gy, dy, ny))

    barrier = pltpu.get_barrier_semaphore()
    greeted = [at(dx, dy) for dx, dy in SIDES] + [(partner, step(gy, d, ny)) for d in PEERS]
    for device in greeted:
        pl.semaphore_signal(barrier, inc=1, device_id=device, device_id_type=MESH)

    local = []
    for index, (src, dst) in enumerate(
        [
            (field, own),
            (cot, cot_own),
            (win_qkv_h, win_qkv),
            (win_out_h, win_out),
            (axial_qkv_h, axial_qkv),
            (axial_out_h, axial_out),
            (mlp_in_h, mlp_in),
            (mlp_out_h, mlp_out),
            (pattern_h, pattern),
        ]
    ):
        copy = pltpu.make_async_copy(src, dst, local_sem.at[index])
        copy.start()
        local.append(copy)
    local[0].wait()
    pl.semaphore_wait(barrier, len(greeted))

    own_y = {0: slice(0, 4), 1: slice(3, 4), -1: slice(0, 1)}
    halo = []
    for index, (dx, dy) in enumerate(SIDES):
        copy = pltpu.make_async_remote_copy(
            src_ref=own.at[:, own_y[dy]],
            dst_ref=sides.at[index - 6] if dy == 0 else edges.at[index],
            send_sem=halo_send.at[index],
            recv_sem=halo_recv.at[index],
            device_id=at(dx, dy),
            device_id_type=MESH,
        )
        copy.start()
        halo.append(copy)

    def exchange(send, recv, group):
        copies = []
        for d in PEERS:
            peer = step(gy, d, ny)
            copy = pltpu.make_async_remote_copy(
                src_ref=send.at[peer],
                dst_ref=recv.at[gy],
                send_sem=a2a_send.at[group, d],
                recv_sem=a2a_recv.at[group, d],
                device_id=(partner, peer),
                device_id_type=MESH,
            )
            copy.start()
            copies.append(copy)
        return copies

    def arrived(send, recv, group):
        for d in PEERS:
            source = step(gy, -d, ny)
            pltpu.make_async_remote_copy(
                src_ref=send.at[source],
                dst_ref=recv.at[source],
                send_sem=a2a_send.at[group, d],
                recv_sem=a2a_recv.at[group, d],
                device_id=(partner, source),
                device_id_type=MESH,
            ).wait_recv()
        return recv[...].reshape(TOK, C)

    row, col = iota((TOK, TOK), 0), iota((TOK, TOK), 1)
    to_zxy = jnp.where(row == (col & 7) * 16 + (col >> 3), 1.0, 0.0).astype(BF16)
    to_xyz = jnp.where(col == (row & 7) * 16 + (row >> 3), 1.0, 0.0).astype(BF16)
    eye = jnp.where(row == col, 1.0, 0.0).astype(BF16)

    local[1].wait()
    cot_send[...] = nn(to_zxy, cot_own[...].reshape(TOK, C)).astype(BF16).reshape(8, 16, C)

    def near(rows, bits, x_base, y_base):
        key, query = iota((rows, TOK), 0), iota((rows, TOK), 1)
        gap_x = (key >> (3 + bits)) + x_base - ((query >> 3) & 1)
        gap_y = ((key >> 3) & ((1 << bits) - 1)) + y_base - (query & 7)
        gap_z = ((key & 7) - (query >> 4) + 2) & 7
        inside = (jnp.abs(gap_x) <= 2) & (jnp.abs(gap_y) <= 2) & (gap_z <= 4)
        return jnp.where(inside, 0.0, MASKED)

    bias1[OWN, :] = near(TOK, 3, 0, 0)
    for index, (dx, dy) in enumerate(SIDES):
        if dy == 0:
            start = 128 * (index - 5)
            bias1[start : start + 128, :] = near(128, 3, -2 * dx, 0)
        else:
            start = 384 + 32 * index
            bias1[start : start + 32, :] = near(32, 1, -2 * dx, -2 if dy == 1 else 8)

    def window_scores(part, tokens):
        values = tokens.astype(F32)
        normed = (values * inverse_rms(values)).astype(BF16)
        kv = nn(normed, win_qkv[:, C : 3 * C]).astype(BF16)
        kv1[part] = kv
        bias = jnp.concatenate([bias1[part, :], bias1[part, :]], axis=1)
        for p in range(PAIRS):
            scores1[p, part] = nt(kv[:, lanes(p)], q1[p]) + bias
            vt1[p, :, part] = nt(eye, kv[:, lanes(p, C)]).astype(BF16)
        return normed

    field_own = own[...].reshape(TOK, C)
    field_zxy = nn(to_zxy, field_own)
    normed1_zxy = (field_zxy * inverse_rms(field_zxy)).astype(BF16)
    local[2].wait()
    query1 = nn(normed1_zxy, win_qkv[:, 0:C]).astype(BF16).astype(F32) * 0.125
    for p in range(PAIRS):
        q1[p] = stacked(query1[:, lanes(p)])
    window_scores(OWN, field_own)
    for copy in halo[6:]:
        copy.wait_recv()
    window_scores(AROUND, sides[...].reshape(256, C))
    tops, sums, outs = [], [], []
    for p in range(PAIRS):
        scores = scores1[p, EARLY]
        tops.append(jnp.max(scores, axis=0, keepdims=True))
        e = jnp.exp(scores - tops[p])
        scores1[p, EARLY] = e
        sums.append(jnp.sum(e, axis=0, keepdims=True))
        outs.append(diagonal(nn(vt1[p, :, EARLY], e.astype(BF16))))
    for copy in halo[:6]:
        copy.wait_recv()
    cot_copies = exchange(cot_send, cot_recv, 0)
    window_scores(EDGES, edges[...].reshape(192, C))
    attended, early_scale = [], []
    for p in range(PAIRS):
        scores = scores1[p, EDGES]
        top = jnp.maximum(tops[p], jnp.max(scores, axis=0, keepdims=True))
        e = jnp.exp(scores - top)
        shrink = jnp.exp(tops[p] - top)
        scale = 1.0 / (shrink * sums[p] + jnp.sum(e, axis=0, keepdims=True))
        weights = (e * scale).astype(BF16)
        weights1[p, EDGES] = weights
        early_scale.append(shrink * scale)
        early = jnp.concatenate(
            [
                outs[p][:64] * early_scale[p][:, :TOK],
                outs[p][64:] * early_scale[p][:, TOK:],
            ],
            axis=0,
        )
        ot = early + diagonal(nn(vt1[p, :, EDGES], weights))
        ot1[p] = ot
        attended.append(nt(eye, ot.astype(BF16)))
    attended = jnp.concatenate(attended, axis=1).astype(BF16)
    local[3].wait()
    s1_send[...] = (field_zxy + nn(attended, win_out[...])).astype(BF16).reshape(8, 16, C)
    s1_copies = exchange(s1_send, s1_recv, 1)

    for p in range(PAIRS):
        weights1[p, EARLY] = (scores1[p, EARLY] * early_scale[p]).astype(BF16)
        kt1[p] = nt(eye, kv1[:, lanes(p)]).astype(BF16)
    for copy in local[4:]:
        copy.wait()
    off = ((col >> 4) - (row >> 4)) & 7
    same_line = ((row ^ col) & 8) == 0
    bias2 = []
    for head in range(2 * PAIRS):
        hit = off == 0
        for j in range(3):
            hit = hit | (off == pattern[j, head])
        bias2.append(jnp.where(hit & same_line, 0.0, MASKED))

    gradient_bf = arrived(cot_send, cot_recv, 0)
    gradient = gradient_bf.astype(F32)
    d_hidden = [
        nt(gradient_bf, mlp_out[512 * c : 512 * (c + 1), :]) for c in range(FF // 512)
    ]
    stream1 = arrived(s1_send, s1_recv, 1).astype(F32)
    r2 = inverse_rms(stream1)
    triple2 = nn((stream1 * r2).astype(BF16), axial_qkv[...]).astype(BF16)
    query2 = triple2[:, 0:C].astype(F32) * 0.125
    q2 = [stacked(query2[:, lanes(p)]) for p in range(PAIRS)]
    weights2 = []
    attended2 = []
    for p in range(PAIRS):
        pair_bias = jnp.concatenate([bias2[2 * p], bias2[2 * p + 1]], axis=0)
        scores = nt(q2[p], triple2[:, lanes(p, C)]) + pair_bias
        e = jnp.exp(scores - jnp.max(scores, axis=1, keepdims=True))
        weights = (e * (1.0 / jnp.sum(e, axis=1, keepdims=True))).astype(BF16)
        weights2.append(weights)
        values = stacked(triple2[:, lanes(p, 2 * C)].astype(F32))
        attended2.append(nn(abreast(weights), values))
    attended2 = jnp.concatenate(attended2, axis=1).astype(BF16)
    stream2 = (stream1 + nn(attended2, axial_out[...])).astype(BF16).astype(F32)

    r3 = inverse_rms(stream2)
    normed3 = (stream2 * r3).astype(BF16)
    hidden = []
    back = None
    for c in range(FF // 512):
        part = slice(512 * c, 512 * (c + 1))
        a = nn(normed3, mlp_in[:, part])
        square = a * a
        t = jnp.tanh(0.7978845608028654 * (a + 0.044715 * (a * square)))
        half = 0.5 * (1.0 + t)
        hidden.append((a * half).astype(BF16))
        slope = half + (0.5 * a) * (1.0 - t * t) * (
            0.7978845608028654 + (3 * 0.044715 * 0.7978845608028654) * square
        )
        term = nt((d_hidden[c] * slope).astype(BF16), mlp_in[:, part])
        back = term if back is None else back + term
    grad2 = gradient + norm_back(stream2, r3, back)

    back2 = nt(grad2.astype(BF16), axial_out[...])
    d_query, d_key, d_value = [], [], []
    for p in range(PAIRS):
        upstream = stacked(back2[:, lanes(p)])
        keys, values = triple2[:, lanes(p, C)], triple2[:, lanes(p, 2 * C)]
        weights = weights2[p].astype(F32)
        d_weights = nt(upstream, values)
        delta = jnp.sum(weights * d_weights, axis=1, keepdims=True)
        d_scores = (weights * (d_weights - delta)).astype(BF16)
        d_query.append(nn(abreast(d_scores), stacked(keys.astype(F32))) * 0.125)
        weights_t = nt(eye, weights2[p])
        d_weights = nt(values, upstream)
        delta = jnp.sum(weights_t * d_weights, axis=0, keepdims=True)
        d_scores = (weights_t * (d_weights - delta)).astype(BF16)
        d_key.append(nn(d_scores, q2[p]))
        d_value.append(nn(weights_t.astype(BF16), upstream))
    d_triple2 = jnp.concatenate(d_query + d_key + d_value, axis=1).astype(BF16)
    grad1 = grad2 + norm_back(stream1, r2, nt(d_triple2, axial_qkv[...]))
    g1_send[...] = grad1.astype(BF16).reshape(8, 16, C)
    g1_copies = exchange(g1_send, g1_recv, 3)

    hidden_out = nn(jnp.concatenate(hidden, axis=1), mlp_out[...])
    lo_send[...] = (stream2 + hidden_out).astype(BF16).reshape(8, 16, C)
    lo_copies = exchange(lo_send, lo_recv, 2)

    grad1_bf = arrived(g1_send, g1_recv, 3)
    back1 = nt(grad1_bf, win_out[...])
    back1_t = nt(win_out[...], grad1_bf).astype(BF16).astype(F32)
    upstream, delta = [], []
    for p in range(PAIRS):
        upstream.append(stacked(back1[:, lanes(p)]))
        product = ot1[p] * back1_t[lanes(p)]
        halves = [jnp.sum(product[h : h + 64], axis=0, keepdims=True) for h in (0, 64)]
        delta.append(jnp.concatenate(halves, axis=1))

    def window_back(part):
        d_scores, d_key, d_value = [], [], []
        for p in range(PAIRS):
            weights = weights1[p, part]
            d_weights = nt(kv1[part, lanes(p, C)], upstream[p])
            d_scores.append((weights.astype(F32) * (d_weights - delta[p])).astype(BF16))
            d_key.append(nn(d_scores[p], q1[p]).astype(BF16))
            d_value.append(nn(weights, upstream[p]).astype(BF16))
        d_kv = jnp.concatenate(d_key + d_value, axis=1)
        return d_scores, nt(d_kv, win_qkv[:, C : 3 * C])

    push = []

    def send_back(index):
        dx, dy = SIDES[index]
        if dy == 0:
            rows = slice(8 * (index - 6), 8 * (index - 5))
        else:
            rows = slice(16 + 2 * index, 18 + 2 * index)
        copy = pltpu.make_async_remote_copy(
            src_ref=dn_send.at[rows],
            dst_ref=dn_recv.at[rows],
            send_sem=push_send.at[index],
            recv_sem=push_recv.at[index],
            device_id=at(-dx, -dy),
            device_id_type=MESH,
        )
        copy.start()
        push.append(copy)

    scores_edges, dn = window_back(EDGES)
    dn_send[16:28] = dn.astype(BF16).reshape(12, 16, C)
    for index in range(6):
        send_back(index)
    scores_around, dn = window_back(AROUND)
    dn_send[0:16] = dn.astype(BF16).reshape(16, 16, C)
    for index in range(6, 8):
        send_back(index)

    scores_own, d_normed = window_back(OWN)
    d_query = []
    for p in range(PAIRS):
        both = nn(kt1[p, :, EDGES], scores_edges[p]) + nn(kt1[p, :, AROUND], scores_around[p])
        both = both + nn(kt1[p, :, OWN], scores_own[p])
        d_query.append((diagonal(both) * 0.125).astype(BF16))
    d_query = nt(to_xyz, jnp.concatenate(d_query, axis=0)).astype(BF16)
    d_normed = d_normed + nt(d_query, win_qkv[:, 0:C])
    grad1_xyz = nn(to_xyz, grad1_bf)
    out_ref[...] = nn(to_xyz, arrived(lo_send, lo_recv, 2)).astype(BF16)
    for copy in push:
        copy.wait_recv()
    d_normed = d_normed + (dn_recv[0:8].astype(F32) + dn_recv[8:16].astype(F32)).reshape(TOK, C)
    first, last = [
        sum(
            dn_recv[16 + 2 * i : 18 + 2 * i].astype(F32)
            for i, (_, dy) in enumerate(SIDES)
            if dy == way
        )
        for way in (-1, 1)
    ]
    none = jnp.zeros((32, C), F32)
    rims = jnp.concatenate([first[0], none, last[0], first[1], none, last[1]], axis=0)
    field_f = own[...].reshape(TOK, C).astype(F32)
    grad_ref[...] = grad1_xyz + norm_back(field_f, inverse_rms(field_f), d_normed + rims)

    for copy in halo + cot_copies + s1_copies + lo_copies + g1_copies + push:
        copy.wait_send()


def store(out_ref, grad_ref, out_hbm, grad_hbm, sem):
    copies = [
        pltpu.make_async_copy(grad_ref, grad_hbm, sem.at[0]),
        pltpu.make_async_copy(out_ref, out_hbm, sem.at[1]),
    ]
    for copy in copies:
        copy.start()
    for copy in copies:
        copy.wait()


def shards(nx, ny, field, cotangent, *rest):
    block = (2, 4, 16, C)
    tiles = (8, 16, C)
    vmem = pltpu.VMEM
    dma = pltpu.SemaphoreType.DMA
    weights, pattern = rest[:6], rest[6]
    in_hbm = pl.BlockSpec(memory_space=pltpu.HBM)
    in_vmem = pl.BlockSpec(memory_space=pltpu.VMEM)
    results = pl.pallas_call(
        functools.partial(kernel, nx, ny),
        out_shape=(pltpu.VMEM((TOK, C), BF16), pltpu.VMEM((TOK, C), F32)),
        in_specs=[in_hbm] * 9,
        out_specs=(in_vmem, in_vmem),
        scratch_shapes=[vmem(w.shape, BF16) for w in weights]
        + [pltpu.SMEM((3, 6), jnp.int32), vmem(block, BF16)]
        + [vmem((2,) + block, BF16), vmem((6, 2, 1, 16, C), BF16)]
        + [vmem(tiles, BF16)] * 9
        + [
            vmem((28, 16, C), BF16),
            vmem((28, 16, C), BF16),
            vmem((PAIRS, KEYS, 256), BF16),
            vmem((KEYS, 2 * C), BF16),
            vmem((PAIRS, TOK, KEYS), BF16),
            vmem((PAIRS, TOK, KEYS), BF16),
            vmem((PAIRS, TOK, TOK), F32),
            vmem((PAIRS, KEYS, 256), F32),
            vmem((KEYS, TOK), F32),
            vmem((PAIRS, 256, TOK), BF16),
            dma((9,)),
            dma((8,)),
            dma((8,)),
            dma((4, 8)),
            dma((4, 8)),
            dma((8,)),
            dma((8,)),
        ],
        compiler_params=pltpu.CompilerParams(
            collective_id=0, has_side_effects=True, vmem_limit_bytes=60 * 1024 * 1024
        ),
    )(field.reshape(block), cotangent.reshape(tiles), *weights, pattern.T)
    layer_output, field_grad = pl.pallas_call(
        store,
        out_shape=(
            jax.ShapeDtypeStruct((TOK, C), BF16),
            jax.ShapeDtypeStruct((TOK, C), F32),
        ),
        in_specs=[in_vmem] * 2,
        out_specs=(in_hbm, in_hbm),
        scratch_shapes=[dma((2,))],
        compiler_params=pltpu.CompilerParams(vmem_limit_bytes=4 * 1024 * 1024),
    )(*results)
    return layer_output.reshape(field.shape), field_grad.reshape(field.shape)


def solution(mesh):
    split = P("gx", "gy", None, None)
    return jax.shard_map(
        functools.partial(shards, mesh.shape["gx"], mesh.shape["gy"]),
        mesh=mesh,
        in_specs=(split, split) + (P(),) * 7,
        out_specs=(split, split),
        check_vma=False,
    )
```

time: 45.8 us -> 38.6 us (0.84)
  Pallas kernels: 41.9 us -> 37.9 us
  local copies, waits for them, and re-layouts: 3.16 us -> 0 us
    pallas_call x1 -> x2, Pallas kernels: 41.9 us -> 37.9 us  [the longest x1 37.2 us: shards(): pl.pallas_call(functools.partial(kernel, nx, ny), out_shape=(pltpu.VMEM((...]
    unnamed x2 -> x0, local copies, waits for them, and re-layouts: 3.16 us -> none
where the time goes in v1:
time: 38.6 us; the launch traced here: 38.5 us
  Pallas kernels  37.9 us (98%)
  between operations  0.64 us (2%)
    pallas_call x1, Pallas kernels, shards(): pl.pallas_call(functools.partial(kernel, nx, ny), out_shape=(pltpu.VMEM((...  37.2 us

profile of v1, /device:TPU:1, one launch (start us, length us, event | category | flops | bytes accessed | tf_op | source)
XLA Modules:
  0.0 38.5 jit_solution(2470948117955551963)
XLA Ops:
  0.6 37.2 %shard_map.104 = (bf16[128,384]{1,0:T(8,128)(2,1)S(1)}, f32[128,384]{1,0:T(8,128)S(1)}) custom-call(bf16[2,4,16,384]{3,2,1,0:T(8,128)(2,1)} %bitcast.5, bf16[8,16,384]{2,1,0:T(8,128)(2,1)} %bitcast.6, bf16[384,1152]{1,0:T(8,128)(2,1)} %win_qkv_h.1, bf16[384,384]{1,0:T(8,128)(2,1)} %win_out_h.1, bf16[384,1152]{1,0:T(8,128)(2,1)} %axial_qkv_h.1, ...), custom_call_target="tpu_custom_call" | custom-call | tf_op jit(solution)/shard_map/pallas_call | solution.py:460
  37.8 0.7 %shard_map.105 = (bf16[128,384]{1,0:T(8,128)(2,1)}, f32[128,384]{1,0:T(8,128)}) custom-call(bf16[128,384]{1,0:T(8,128)(2,1)S(1)} %get-tuple-element.6.out_ref, f32[128,384]{1,0:T(8,128)S(1)} %get-tuple-element.7.grad_ref), custom_call_target="tpu_custom_call" | custom-call | tf_op jit(solution)/shard_map/pallas_call | solution.py:492

commit v2 on v1

--- a/solution.py
+++ b/solution.py
@@ -82,6 +82,11 @@
     axial_out,
     mlp_in,
     mlp_out,
+    win_out_t,
+    win_kv_t,
+    axial_out_t,
+    axial_qkv_t,
+    mlp_in_t,
     pattern,
     own,
     sides,
@@ -239,6 +244,11 @@
     for p in range(PAIRS):
         q1[p] = stacked(query1[:, lanes(p)])
     window_scores(OWN, field_own)
+    cot_copies = exchange(cot_send, cot_recv, 0)
+    for copy in local[5:7]:
+        copy.wait()
+    axial_out_t[...] = axial_out[...].T
+    mlp_in_t[...] = mlp_in[...].T
     for copy in halo[6:]:
         copy.wait_recv()
     window_scores(AROUND, sides[...].reshape(256, C))
@@ -252,7 +262,6 @@
         outs.append(diagonal(nn(vt1[p, :, EARLY], e.astype(BF16))))
     for copy in halo[:6]:
         copy.wait_recv()
-    cot_copies = exchange(cot_send, cot_recv, 0)
     window_scores(EDGES, edges[...].reshape(192, C))
     attended, early_scale = [], []
     for p in range(PAIRS):
@@ -273,8 +282,8 @@
         )
         ot = early + diagonal(nn(vt1[p, :, EDGES], weights))
         ot1[p] = ot
-        attended.append(nt(eye, ot.astype(BF16)))
-    attended = jnp.concatenate(attended, axis=1).astype(BF16)
+        attended.append(ot.astype(BF16).T)
+    attended = jnp.concatenate(attended, axis=1)
     local[3].wait()
     s1_send[...] = (field_zxy + nn(attended, win_out[...])).astype(BF16).reshape(8, 16, C)
     s1_copies = exchange(s1_send, s1_recv, 1)
@@ -282,8 +291,9 @@
     for p in range(PAIRS):
         weights1[p, EARLY] = (scores1[p, EARLY] * early_scale[p]).astype(BF16)
         kt1[p] = nt(eye, kv1[:, lanes(p)]).astype(BF16)
-    for copy in local[4:]:
+    for copy in (local[4], local[7], local[8]):
         copy.wait()
+    axial_qkv_t[...] = axial_qkv[...].T
     off = ((col >> 4) - (row >> 4)) & 7
     same_line = ((row ^ col) & 8) == 0
     bias2 = []
@@ -330,37 +340,35 @@
         slope = half + (0.5 * a) * (1.0 - t * t) * (
             0.7978845608028654 + (3 * 0.044715 * 0.7978845608028654) * square
         )
-        term = nt((d_hidden[c] * slope).astype(BF16), mlp_in[:, part])
+        term = nn((d_hidden[c] * slope).astype(BF16), mlp_in_t[part, :])
         back = term if back is None else back + term
     grad2 = gradient + norm_back(stream2, r3, back)
 
-    back2 = nt(grad2.astype(BF16), axial_out[...])
+    back2 = nn(grad2.astype(BF16), axial_out_t[...])
     d_query, d_key, d_value = [], [], []
     for p in range(PAIRS):
         upstream = stacked(back2[:, lanes(p)])
-        keys, values = triple2[:, lanes(p, C)], triple2[:, lanes(p, 2 * C)]
+        keys = stacked(triple2[:, lanes(p, C)].astype(F32))
         weights = weights2[p].astype(F32)
-        d_weights = nt(upstream, values)
+        d_weights = nt(upstream, triple2[:, lanes(p, 2 * C)])
         delta = jnp.sum(weights * d_weights, axis=1, keepdims=True)
         d_scores = (weights * (d_weights - delta)).astype(BF16)
-        d_query.append(nn(abreast(d_scores), stacked(keys.astype(F32))) * 0.125)
-        weights_t = nt(eye, weights2[p])
-        d_weights = nt(values, upstream)
-        delta = jnp.sum(weights_t * d_weights, axis=0, keepdims=True)
-        d_scores = (weights_t * (d_weights - delta)).astype(BF16)
-        d_key.append(nn(d_scores, q2[p]))
-        d_value.append(nn(weights_t.astype(BF16), upstream))
+        d_query.append(nn(abreast(d_scores), keys) * 0.125)
+        d_key.append(nn(d_scores.T, q2[p]))
+        d_value.append(nn(weights2[p].T, upstream))
     d_triple2 = jnp.concatenate(d_query + d_key + d_value, axis=1).astype(BF16)
-    grad1 = grad2 + norm_back(stream1, r2, nt(d_triple2, axial_qkv[...]))
+    grad1 = grad2 + norm_back(stream1, r2, nn(d_triple2, axial_qkv_t[...]))
     g1_send[...] = grad1.astype(BF16).reshape(8, 16, C)
     g1_copies = exchange(g1_send, g1_recv, 3)
 
     hidden_out = nn(jnp.concatenate(hidden, axis=1), mlp_out[...])
     lo_send[...] = (stream2 + hidden_out).astype(BF16).reshape(8, 16, C)
     lo_copies = exchange(lo_send, lo_recv, 2)
+    win_out_t[...] = win_out[...].T
+    win_kv_t[...] = win_qkv[:, C : 3 * C].T
 
     grad1_bf = arrived(g1_send, g1_recv, 3)
-    back1 = nt(grad1_bf, win_out[...])
+    back1 = nn(grad1_bf, win_out_t[...])
     back1_t = nt(win_out[...], grad1_bf).astype(BF16).astype(F32)
     upstream, delta = [], []
     for p in range(PAIRS):
@@ -378,7 +386,7 @@
             d_key.append(nn(d_scores[p], q1[p]).astype(BF16))
             d_value.append(nn(weights, upstream[p]).astype(BF16))
         d_kv = jnp.concatenate(d_key + d_value, axis=1)
-        return d_scores, nt(d_kv, win_qkv[:, C : 3 * C])
+        return d_scores, nn(d_kv, win_kv_t[...])
 
     push = []
 
@@ -463,6 +471,7 @@
         in_specs=[in_hbm] * 9,
         out_specs=(in_vmem, in_vmem),
         scratch_shapes=[vmem(w.shape, BF16) for w in weights]
+        + [vmem((n, C), BF16) for n in (C, 2 * C, C, 3 * C, FF)]
         + [pltpu.SMEM((3, 6), jnp.int32), vmem(block, BF16)]
         + [vmem((2,) + block, BF16), vmem((6, 2, 1, 16, C), BF16)]
         + [vmem(tiles, BF16)] * 9

time: 38.6 us -> 37.8 us (0.979)
  Pallas kernels: 37.9 us -> 37 us
    pallas_call x1, Pallas kernels: 37.2 us -> 36.3 us  [shards(): pl.pallas_call(functools.partial(kernel, nx, ny), out_shape=(pltpu.VMEM((...]
where the time goes in v2:
time: 37.8 us; the launch traced here: 37.7 us
  Pallas kernels  37 us (98%)
  between operations  0.64 us (2%)
    pallas_call x1, Pallas kernels, shards(): pl.pallas_call(functools.partial(kernel, nx, ny), out_shape=(pltpu.VMEM((...  36.3 us

profile of v2, /device:TPU:1, one launch (start us, length us, event | category | flops | bytes accessed | tf_op | source)
XLA Modules:
  0.0 37.7 jit_solution(8935093022835511869)
XLA Ops:
  0.6 36.3 %shard_map.104 = (bf16[128,384]{1,0:T(8,128)(2,1)S(1)}, f32[128,384]{1,0:T(8,128)S(1)}) custom-call(bf16[2,4,16,384]{3,2,1,0:T(8,128)(2,1)} %bitcast.5, bf16[8,16,384]{2,1,0:T(8,128)(2,1)} %bitcast.6, bf16[384,1152]{1,0:T(8,128)(2,1)} %win_qkv_h.1, bf16[384,384]{1,0:T(8,128)(2,1)} %win_out_h.1, bf16[384,1152]{1,0:T(8,128)(2,1)} %axial_qkv_h.1, ...), custom_call_target="tpu_custom_call" | custom-call | tf_op jit(solution)/shard_map/pallas_call | solution.py:468
  37.0 0.7 %shard_map.105 = (bf16[128,384]{1,0:T(8,128)(2,1)}, f32[128,384]{1,0:T(8,128)}) custom-call(bf16[128,384]{1,0:T(8,128)(2,1)S(1)} %get-tuple-element.6.out_ref, f32[128,384]{1,0:T(8,128)S(1)} %get-tuple-element.7.grad_ref), custom_call_target="tpu_custom_call" | custom-call | tf_op jit(solution)/shard_map/pallas_call | solution.py:501

commit v3 on v2

--- a/solution.py
+++ b/solution.py
@@ -11,6 +11,7 @@
 BF16 = jnp.bfloat16
 C = 384
 FF = 1536
+CHUNK = 1536
 PAIRS = 3
 TOK = 128
 KEYS = 576
@@ -42,12 +43,6 @@
 
 def iota(shape, dim):
     return lax.broadcasted_iota(jnp.int32, shape, dim)
-
-
-def stacked(pair):
-    first = iota(pair.shape, 1) < 64
-    upper = jnp.where(first, pair, 0.0)
-    return jnp.concatenate([upper, pair - upper], axis=0).astype(BF16)
 
 
 def diagonal(both):
@@ -204,6 +199,11 @@
     to_zxy = jnp.where(row == (col & 7) * 16 + (col >> 3), 1.0, 0.0).astype(BF16)
     to_xyz = jnp.where(col == (row & 7) * 16 + (row >> 3), 1.0, 0.0).astype(BF16)
     eye = jnp.where(row == col, 1.0, 0.0).astype(BF16)
+    head0 = jnp.where(col < 64, 1.0, 0.0).astype(BF16)
+    head1 = jnp.where(col < 64, 0.0, 1.0).astype(BF16)
+
+    def stacked(pair):
+        return jnp.concatenate([pair * head0, pair * head1], axis=0)
 
     local[1].wait()
     cot_send[...] = nn(to_zxy, cot_own[...].reshape(TOK, C)).astype(BF16).reshape(8, 16, C)
@@ -240,7 +240,7 @@
     field_zxy = nn(to_zxy, field_own)
     normed1_zxy = (field_zxy * inverse_rms(field_zxy)).astype(BF16)
     local[2].wait()
-    query1 = nn(normed1_zxy, win_qkv[:, 0:C]).astype(BF16).astype(F32) * 0.125
+    query1 = nn(normed1_zxy, win_qkv[:, 0:C]).astype(BF16) * 0.125
     for p in range(PAIRS):
         q1[p] = stacked(query1[:, lanes(p)])
     window_scores(OWN, field_own)
@@ -306,12 +306,12 @@
     gradient_bf = arrived(cot_send, cot_recv, 0)
     gradient = gradient_bf.astype(F32)
     d_hidden = [
-        nt(gradient_bf, mlp_out[512 * c : 512 * (c + 1), :]) for c in range(FF // 512)
+        nt(gradient_bf, mlp_out[CHUNK * c : CHUNK * (c + 1), :]) for c in range(FF // CHUNK)
     ]
     stream1 = arrived(s1_send, s1_recv, 1).astype(F32)
     r2 = inverse_rms(stream1)
     triple2 = nn((stream1 * r2).astype(BF16), axial_qkv[...]).astype(BF16)
-    query2 = triple2[:, 0:C].astype(F32) * 0.125
+    query2 = triple2[:, 0:C] * 0.125
     q2 = [stacked(query2[:, lanes(p)]) for p in range(PAIRS)]
     weights2 = []
     attended2 = []
@@ -321,7 +321,7 @@
         e = jnp.exp(scores - jnp.max(scores, axis=1, keepdims=True))
         weights = (e * (1.0 / jnp.sum(e, axis=1, keepdims=True))).astype(BF16)
         weights2.append(weights)
-        values = stacked(triple2[:, lanes(p, 2 * C)].astype(F32))
+        values = stacked(triple2[:, lanes(p, 2 * C)])
         attended2.append(nn(abreast(weights), values))
     attended2 = jnp.concatenate(attended2, axis=1).astype(BF16)
     stream2 = (stream1 + nn(attended2, axial_out[...])).astype(BF16).astype(F32)
@@ -330,8 +330,8 @@
     normed3 = (stream2 * r3).astype(BF16)
     hidden = []
     back = None
-    for c in range(FF // 512):
-        part = slice(512 * c, 512 * (c + 1))
+    for c in range(FF // CHUNK):
+        part = slice(CHUNK * c, CHUNK * (c + 1))
         a = nn(normed3, mlp_in[:, part])
         square = a * a
         t = jnp.tanh(0.7978845608028654 * (a + 0.044715 * (a * square)))
@@ -344,11 +344,11 @@
         back = term if back is None else back + term
     grad2 = gradient + norm_back(stream2, r3, back)
 
-    back2 = nn(grad2.astype(BF16), axial_out_t[...])
+    back2 = nn(grad2.astype(BF16), axial_out_t[...]).astype(BF16)
     d_query, d_key, d_value = [], [], []
     for p in range(PAIRS):
         upstream = stacked(back2[:, lanes(p)])
-        keys = stacked(triple2[:, lanes(p, C)].astype(F32))
+        keys = stacked(triple2[:, lanes(p, C)])
         weights = weights2[p].astype(F32)
         d_weights = nt(upstream, triple2[:, lanes(p, 2 * C)])
         delta = jnp.sum(weights * d_weights, axis=1, keepdims=True)
@@ -368,7 +368,7 @@
     win_kv_t[...] = win_qkv[:, C : 3 * C].T
 
     grad1_bf = arrived(g1_send, g1_recv, 3)
-    back1 = nn(grad1_bf, win_out_t[...])
+    back1 = nn(grad1_bf, win_out_t[...]).astype(BF16)
     back1_t = nt(win_out[...], grad1_bf).astype(BF16).astype(F32)
     upstream, delta = [], []
     for p in range(PAIRS):
@@ -407,13 +407,11 @@
         copy.start()
         push.append(copy)
 
-    scores_edges, dn = window_back(EDGES)
-    dn_send[16:28] = dn.astype(BF16).reshape(12, 16, C)
-    for index in range(6):
-        send_back(index)
-    scores_around, dn = window_back(AROUND)
-    dn_send[0:16] = dn.astype(BF16).reshape(16, 16, C)
-    for index in range(6, 8):
+    scores_edges, dn_edges = window_back(EDGES)
+    scores_around, dn_around = window_back(AROUND)
+    dn_send[16:28] = dn_edges.astype(BF16).reshape(12, 16, C)
+    dn_send[0:16] = dn_around.astype(BF16).reshape(16, 16, C)
+    for index in range(8):
         send_back(index)
 
     scores_own, d_normed = window_back(OWN)

time: 37.8 us -> 38.4 us (1.016)
  Pallas kernels: 37 us -> 37.7 us
    pallas_call x1, Pallas kernels: 36.3 us -> 37 us  [shards(): pl.pallas_call(functools.partial(kernel, nx, ny), out_shape=(pltpu.VMEM((...]
where the time goes in v3:
time: 38.4 us; the launch traced here: 38.3 us
  Pallas kernels  37.7 us (98%)
  between operations  0.64 us (2%)
    pallas_call x1, Pallas kernels, shards(): pl.pallas_call(functools.partial(kernel, nx, ny), out_shape=(pltpu.VMEM((...  37 us

profile of v3, /device:TPU:1, one launch (start us, length us, event | category | flops | bytes accessed | tf_op | source)
XLA Modules:
  0.0 38.3 jit_solution(15229159533063231897)
XLA Ops:
  0.6 37.0 %shard_map.104 = (bf16[128,384]{1,0:T(8,128)(2,1)S(1)}, f32[128,384]{1,0:T(8,128)S(1)}) custom-call(bf16[2,4,16,384]{3,2,1,0:T(8,128)(2,1)} %bitcast.5, bf16[8,16,384]{2,1,0:T(8,128)(2,1)} %bitcast.6, bf16[384,1152]{1,0:T(8,128)(2,1)} %win_qkv_h.1, bf16[384,384]{1,0:T(8,128)(2,1)} %win_out_h.1, bf16[384,1152]{1,0:T(8,128)(2,1)} %axial_qkv_h.1, ...), custom_call_target="tpu_custom_call" | custom-call | tf_op jit(solution)/shard_map/pallas_call | solution.py:466
  37.6 0.7 %shard_map.105 = (bf16[128,384]{1,0:T(8,128)(2,1)}, f32[128,384]{1,0:T(8,128)}) custom-call(bf16[128,384]{1,0:T(8,128)(2,1)S(1)} %get-tuple-element.6.out_ref, f32[128,384]{1,0:T(8,128)S(1)} %get-tuple-element.7.grad_ref), custom_call_target="tpu_custom_call" | custom-call | tf_op jit(solution)/shard_map/pallas_call | solution.py:499

commit v4 on v3

--- a/solution.py
+++ b/solution.py
@@ -132,23 +132,24 @@
     for device in greeted:
         pl.semaphore_signal(barrier, inc=1, device_id=device, device_id_type=MESH)
 
-    local = []
-    for index, (src, dst) in enumerate(
-        [
-            (field, own),
-            (cot, cot_own),
-            (win_qkv_h, win_qkv),
-            (win_out_h, win_out),
-            (axial_qkv_h, axial_qkv),
-            (axial_out_h, axial_out),
-            (mlp_in_h, mlp_in),
-            (mlp_out_h, mlp_out),
-            (pattern_h, pattern),
-        ]
-    ):
-        copy = pltpu.make_async_copy(src, dst, local_sem.at[index])
+    local = [
+        pltpu.make_async_copy(src, dst, local_sem.at[index])
+        for index, (src, dst) in enumerate(
+            [
+                (field, own),
+                (cot, cot_own),
+                (win_qkv_h, win_qkv),
+                (win_out_h, win_out),
+                (axial_qkv_h, axial_qkv),
+                (axial_out_h, axial_out),
+                (mlp_in_h, mlp_in),
+                (mlp_out_h, mlp_out),
+                (pattern_h, pattern),
+            ]
+        )
+    ]
+    for copy in local[:2]:
         copy.start()
-        local.append(copy)
     local[0].wait()
     pl.semaphore_wait(barrier, len(greeted))
 
@@ -165,6 +166,8 @@
         )
         copy.start()
         halo.append(copy)
+    for copy in local[2:]:
+        copy.start()
 
     def exchange(send, recv, group):
         copies = []
@@ -407,11 +410,13 @@
         copy.start()
         push.append(copy)
 
-    scores_edges, dn_edges = window_back(EDGES)
-    scores_around, dn_around = window_back(AROUND)
-    dn_send[16:28] = dn_edges.astype(BF16).reshape(12, 16, C)
-    dn_send[0:16] = dn_around.astype(BF16).reshape(16, 16, C)
-    for index in range(8):
+    scores_edges, dn = window_back(EDGES)
+    dn_send[16:28] = dn.astype(BF16).reshape(12, 16, C)
+    for index in range(6):
+        send_back(index)
+    scores_around, dn = window_back(AROUND)
+    dn_send[0:16] = dn.astype(BF16).reshape(16, 16, C)
+    for index in range(6, 8):
         send_back(index)
 
     scores_own, d_normed = window_back(OWN)

time: 38.4 us -> 37.7 us (0.982)
  Pallas kernels: 37.7 us -> 36.9 us
    pallas_call x1, Pallas kernels: 37 us -> 36.2 us  [shards(): pl.pallas_call(functools.partial(kernel, nx, ny), out_shape=(pltpu.VMEM((...]
where the time goes in v4:
time: 37.7 us; the launch traced here: 37.5 us
  Pallas kernels  36.9 us (98%)
  between operations  0.64 us (2%)
    pallas_call x1, Pallas kernels, shards(): pl.pallas_call(functools.partial(kernel, nx, ny), out_shape=(pltpu.VMEM((...  36.2 us

profile of v4, /device:TPU:1, one launch (start us, length us, event | category | flops | bytes accessed | tf_op | source)
XLA Modules:
  0.0 37.5 jit_solution(11778384921930571614)
XLA Ops:
  0.6 36.2 %shard_map.104 = (bf16[128,384]{1,0:T(8,128)(2,1)S(1)}, f32[128,384]{1,0:T(8,128)S(1)}) custom-call(bf16[2,4,16,384]{3,2,1,0:T(8,128)(2,1)} %bitcast.5, bf16[8,16,384]{2,1,0:T(8,128)(2,1)} %bitcast.6, bf16[384,1152]{1,0:T(8,128)(2,1)} %win_qkv_h.1, bf16[384,384]{1,0:T(8,128)(2,1)} %win_out_h.1, bf16[384,1152]{1,0:T(8,128)(2,1)} %axial_qkv_h.1, ...), custom_call_target="tpu_custom_call" | custom-call | tf_op jit(solution)/shard_map/pallas_call | solution.py:471
  36.8 0.7 %shard_map.105 = (bf16[128,384]{1,0:T(8,128)(2,1)}, f32[128,384]{1,0:T(8,128)}) custom-call(bf16[128,384]{1,0:T(8,128)(2,1)S(1)} %get-tuple-element.6.out_ref, f32[128,384]{1,0:T(8,128)S(1)} %get-tuple-element.7.grad_ref), custom_call_target="tpu_custom_call" | custom-call | tf_op jit(solution)/shard_map/pallas_call | solution.py:504

commit v5 on v4

--- a/solution.py
+++ b/solution.py
@@ -11,11 +11,12 @@
 BF16 = jnp.bfloat16
 C = 384
 FF = 1536
-CHUNK = 1536
+CHUNK = 512
 PAIRS = 3
 TOK = 128
 KEYS = 576
-OWN, AROUND, EARLY, EDGES = slice(0, 128), slice(128, 384), slice(0, 384), slice(384, 576)
+OWN, EDGES, AROUND, EARLY = slice(0, 128), slice(128, 320), slice(320, 576), slice(0, 320)
+OWN_LANES, AROUND_LANES, EDGES_LANES = slice(0, 128), slice(128, 384), slice(384, 576)
 EPSILON = 1e-06
 MASKED = -1e30
 MESH = pl.DeviceIdType.MESH
@@ -222,13 +223,13 @@
     bias1[OWN, :] = near(TOK, 3, 0, 0)
     for index, (dx, dy) in enumerate(SIDES):
         if dy == 0:
-            start = 128 * (index - 5)
+            start = 320 + 128 * (index - 6)
             bias1[start : start + 128, :] = near(128, 3, -2 * dx, 0)
         else:
-            start = 384 + 32 * index
+            start = 128 + 32 * index
             bias1[start : start + 32, :] = near(32, 1, -2 * dx, -2 if dy == 1 else 8)
 
-    def window_scores(part, tokens):
+    def window_scores(part, part_lanes, tokens):
         values = tokens.astype(F32)
         normed = (values * inverse_rms(values)).astype(BF16)
         kv = nn(normed, win_qkv[:, C : 3 * C]).astype(BF16)
@@ -236,8 +237,7 @@
         bias = jnp.concatenate([bias1[part, :], bias1[part, :]], axis=1)
         for p in range(PAIRS):
             scores1[p, part] = nt(kv[:, lanes(p)], q1[p]) + bias
-            vt1[p, :, part] = nt(eye, kv[:, lanes(p, C)]).astype(BF16)
-        return normed
+            vt1[p, :, part_lanes] = nt(eye, kv[:, lanes(p, C)]).astype(BF16)
 
     field_own = own[...].reshape(TOK, C)
     field_zxy = nn(to_zxy, field_own)
@@ -246,15 +246,15 @@
     query1 = nn(normed1_zxy, win_qkv[:, 0:C]).astype(BF16) * 0.125
     for p in range(PAIRS):
         q1[p] = stacked(query1[:, lanes(p)])
-    window_scores(OWN, field_own)
+    window_scores(OWN, OWN_LANES, field_own)
     cot_copies = exchange(cot_send, cot_recv, 0)
     for copy in local[5:7]:
         copy.wait()
     axial_out_t[...] = axial_out[...].T
     mlp_in_t[...] = mlp_in[...].T
-    for copy in halo[6:]:
+    for copy in halo[:6]:
         copy.wait_recv()
-    window_scores(AROUND, sides[...].reshape(256, C))
+    window_scores(EDGES, EDGES_LANES, edges[...].reshape(192, C))
     tops, sums, outs = [], [], []
     for p in range(PAIRS):
         scores = scores1[p, EARLY]
@@ -262,19 +262,21 @@
         e = jnp.exp(scores - tops[p])
         scores1[p, EARLY] = e
         sums.append(jnp.sum(e, axis=0, keepdims=True))
-        outs.append(diagonal(nn(vt1[p, :, EARLY], e.astype(BF16))))
-    for copy in halo[:6]:
+        e = e.astype(BF16)
+        out = nn(vt1[p, :, OWN_LANES], e[OWN]) + nn(vt1[p, :, EDGES_LANES], e[EDGES])
+        outs.append(diagonal(out))
+    for copy in halo[6:]:
         copy.wait_recv()
-    window_scores(EDGES, edges[...].reshape(192, C))
+    window_scores(AROUND, AROUND_LANES, sides[...].reshape(256, C))
     attended, early_scale = [], []
     for p in range(PAIRS):
-        scores = scores1[p, EDGES]
+        scores = scores1[p, AROUND]
         top = jnp.maximum(tops[p], jnp.max(scores, axis=0, keepdims=True))
         e = jnp.exp(scores - top)
         shrink = jnp.exp(tops[p] - top)
         scale = 1.0 / (shrink * sums[p] + jnp.sum(e, axis=0, keepdims=True))
         weights = (e * scale).astype(BF16)
-        weights1[p, EDGES] = weights
+        weights1[p, AROUND] = weights
         early_scale.append(shrink * scale)
         early = jnp.concatenate(
             [
@@ -283,7 +285,7 @@
             ],
             axis=0,
         )
-        ot = early + diagonal(nn(vt1[p, :, EDGES], weights))
+        ot = early + diagonal(nn(vt1[p, :, AROUND_LANES], weights))
         ot1[p] = ot
         attended.append(ot.astype(BF16).T)
     attended = jnp.concatenate(attended, axis=1)
@@ -293,7 +295,12 @@
 
     for p in range(PAIRS):
         weights1[p, EARLY] = (scores1[p, EARLY] * early_scale[p]).astype(BF16)
-        kt1[p] = nt(eye, kv1[:, lanes(p)]).astype(BF16)
+        for part, part_lanes in (
+            (OWN, OWN_LANES),
+            (AROUND, AROUND_LANES),
+            (EDGES, EDGES_LANES),
+        ):
+            kt1[p, :, part_lanes] = nt(eye, kv1[part, lanes(p)]).astype(BF16)
     for copy in (local[4], local[7], local[8]):
         copy.wait()
     axial_qkv_t[...] = axial_qkv[...].T
@@ -308,9 +315,7 @@
 
     gradient_bf = arrived(cot_send, cot_recv, 0)
     gradient = gradient_bf.astype(F32)
-    d_hidden = [
-        nt(gradient_bf, mlp_out[CHUNK * c : CHUNK * (c + 1), :]) for c in range(FF // CHUNK)
-    ]
+    d_hidden = nt(gradient_bf, mlp_out[...])
     stream1 = arrived(s1_send, s1_recv, 1).astype(F32)
     r2 = inverse_rms(stream1)
     triple2 = nn((stream1 * r2).astype(BF16), axial_qkv[...]).astype(BF16)
@@ -331,20 +336,18 @@
 
     r3 = inverse_rms(stream2)
     normed3 = (stream2 * r3).astype(BF16)
-    hidden = []
-    back = None
+    hidden, d_inner = [], []
     for c in range(FF // CHUNK):
         part = slice(CHUNK * c, CHUNK * (c + 1))
         a = nn(normed3, mlp_in[:, part])
         square = a * a
-        t = jnp.tanh(0.7978845608028654 * (a + 0.044715 * (a * square)))
-        half = 0.5 * (1.0 + t)
+        t = jnp.tanh(a * (0.7978845608028654 + (0.044715 * 0.7978845608028654) * square))
+        half = 0.5 + 0.5 * t
         hidden.append((a * half).astype(BF16))
-        slope = half + (0.5 * a) * (1.0 - t * t) * (
-            0.7978845608028654 + (3 * 0.044715 * 0.7978845608028654) * square
-        )
-        term = nn((d_hidden[c] * slope).astype(BF16), mlp_in_t[part, :])
-        back = term if back is None else back + term
+        steep = a * (2 * 0.7978845608028654 + (6 * 0.044715 * 0.7978845608028654) * square)
+        slope = half + (half - half * half) * steep
+        d_inner.append((d_hidden[:, part] * slope).astype(BF16))
+    back = nn(jnp.concatenate(d_inner, axis=1), mlp_in_t[...])
     grad2 = gradient + norm_back(stream2, r3, back)
 
     back2 = nn(grad2.astype(BF16), axial_out_t[...]).astype(BF16)
@@ -368,7 +371,8 @@
     lo_send[...] = (stream2 + hidden_out).astype(BF16).reshape(8, 16, C)
     lo_copies = exchange(lo_send, lo_recv, 2)
     win_out_t[...] = win_out[...].T
-    win_kv_t[...] = win_qkv[:, C : 3 * C].T
+    win_kv_t[0:C] = win_qkv[:, 2 * C : 3 * C].T
+    win_kv_t[C : 2 * C] = win_qkv[:, C : 2 * C].T
 
     grad1_bf = arrived(g1_send, g1_recv, 3)
     back1 = nn(grad1_bf, win_out_t[...]).astype(BF16)
@@ -388,7 +392,7 @@
             d_scores.append((weights.astype(F32) * (d_weights - delta[p])).astype(BF16))
             d_key.append(nn(d_scores[p], q1[p]).astype(BF16))
             d_value.append(nn(weights, upstream[p]).astype(BF16))
-        d_kv = jnp.concatenate(d_key + d_value, axis=1)
+        d_kv = jnp.concatenate(d_value + d_key, axis=1)
         return d_scores, nn(d_kv, win_kv_t[...])
 
     push = []
@@ -422,8 +426,9 @@
     scores_own, d_normed = window_back(OWN)
     d_query = []
     for p in range(PAIRS):
-        both = nn(kt1[p, :, EDGES], scores_edges[p]) + nn(kt1[p, :, AROUND], scores_around[p])
-        both = both + nn(kt1[p, :, OWN], scores_own[p])
+        both = nn(kt1[p, :, EDGES_LANES], scores_edges[p])
+        both = both + nn(kt1[p, :, AROUND_LANES], scores_around[p])
+        both = both + nn(kt1[p, :, OWN_LANES], scores_own[p])
         d_query.append((diagonal(both) * 0.125).astype(BF16))
     d_query = nt(to_xyz, jnp.concatenate(d_query, axis=0)).astype(BF16)
     d_normed = d_normed + nt(d_query, win_qkv[:, 0:C])

time: 37.7 us -> 38.6 us (1.024)
  Pallas kernels: 36.9 us -> 37.8 us
    pallas_call x1, Pallas kernels: 36.2 us -> 37.1 us  [shards(): pl.pallas_call(functools.partial(kernel, nx, ny), out_shape=(pltpu.VMEM((...]
where the time goes in v5:
time: 38.6 us; the launch traced here: 38.4 us
  Pallas kernels  37.8 us (98%)
  between operations  0.64 us (2%)
    pallas_call x1, Pallas kernels, shards(): pl.pallas_call(functools.partial(kernel, nx, ny), out_shape=(pltpu.VMEM((...  37.1 us

profile of v5, /device:TPU:1, one launch (start us, length us, event | category | flops | bytes accessed | tf_op | source)
XLA Modules:
  0.0 38.4 jit_solution(10570059492854165066)
XLA Ops:
  0.6 37.1 %shard_map.104 = (bf16[128,384]{1,0:T(8,128)(2,1)S(1)}, f32[128,384]{1,0:T(8,128)S(1)}) custom-call(bf16[2,4,16,384]{3,2,1,0:T(8,128)(2,1)} %bitcast.5, bf16[8,16,384]{2,1,0:T(8,128)(2,1)} %bitcast.6, bf16[384,1152]{1,0:T(8,128)(2,1)} %win_qkv_h.1, bf16[384,384]{1,0:T(8,128)(2,1)} %win_out_h.1, bf16[384,1152]{1,0:T(8,128)(2,1)} %axial_qkv_h.1, ...), custom_call_target="tpu_custom_call" | custom-call | tf_op jit(solution)/shard_map/pallas_call | solution.py:476
  37.7 0.7 %shard_map.105 = (bf16[128,384]{1,0:T(8,128)(2,1)}, f32[128,384]{1,0:T(8,128)}) custom-call(bf16[128,384]{1,0:T(8,128)(2,1)S(1)} %get-tuple-element.6.out_ref, f32[128,384]{1,0:T(8,128)S(1)} %get-tuple-element.7.grad_ref), custom_call_target="tpu_custom_call" | custom-call | tf_op jit(solution)/shard_map/pallas_call | solution.py:509

commit v6 on v4

--- a/solution.py
+++ b/solution.py
@@ -11,7 +11,7 @@
 BF16 = jnp.bfloat16
 C = 384
 FF = 1536
-CHUNK = 1536
+CHUNK = 512
 PAIRS = 3
 TOK = 128
 KEYS = 576
@@ -164,8 +164,9 @@
             device_id=at(dx, dy),
             device_id_type=MESH,
         )
+        halo.append(copy)
+    for copy in halo[:6]:
         copy.start()
-        halo.append(copy)
     for copy in local[2:]:
         copy.start()
 
@@ -228,6 +229,9 @@
             start = 384 + 32 * index
             bias1[start : start + 32, :] = near(32, 1, -2 * dx, -2 if dy == 1 else 8)
 
+    for copy in halo[6:]:
+        copy.start()
+
     def window_scores(part, tokens):
         values = tokens.astype(F32)
         normed = (values * inverse_rms(values)).astype(BF16)
@@ -247,7 +251,6 @@
     for p in range(PAIRS):
         q1[p] = stacked(query1[:, lanes(p)])
     window_scores(OWN, field_own)
-    cot_copies = exchange(cot_send, cot_recv, 0)
     for copy in local[5:7]:
         copy.wait()
     axial_out_t[...] = axial_out[...].T
@@ -265,6 +268,7 @@
         outs.append(diagonal(nn(vt1[p, :, EARLY], e.astype(BF16))))
     for copy in halo[:6]:
         copy.wait_recv()
+    cot_copies = exchange(cot_send, cot_recv, 0)
     window_scores(EDGES, edges[...].reshape(192, C))
     attended, early_scale = [], []
     for p in range(PAIRS):
@@ -308,9 +312,7 @@
 
     gradient_bf = arrived(cot_send, cot_recv, 0)
     gradient = gradient_bf.astype(F32)
-    d_hidden = [
-        nt(gradient_bf, mlp_out[CHUNK * c : CHUNK * (c + 1), :]) for c in range(FF // CHUNK)
-    ]
+    d_hidden = nt(gradient_bf, mlp_out[...])
     stream1 = arrived(s1_send, s1_recv, 1).astype(F32)
     r2 = inverse_rms(stream1)
     triple2 = nn((stream1 * r2).astype(BF16), axial_qkv[...]).astype(BF16)
@@ -331,20 +333,18 @@
 
     r3 = inverse_rms(stream2)
     normed3 = (stream2 * r3).astype(BF16)
-    hidden = []
-    back = None
+    hidden, d_inner = [], []
     for c in range(FF // CHUNK):
         part = slice(CHUNK * c, CHUNK * (c + 1))
         a = nn(normed3, mlp_in[:, part])
         square = a * a
-        t = jnp.tanh(0.7978845608028654 * (a + 0.044715 * (a * square)))
-        half = 0.5 * (1.0 + t)
+        t = jnp.tanh(a * (0.7978845608028654 + (0.044715 * 0.7978845608028654) * square))
+        half = 0.5 + 0.5 * t
         hidden.append((a * half).astype(BF16))
-        slope = half + (0.5 * a) * (1.0 - t * t) * (
-            0.7978845608028654 + (3 * 0.044715 * 0.7978845608028654) * square
-        )
-        term = nn((d_hidden[c] * slope).astype(BF16), mlp_in_t[part, :])
-        back = term if back is None else back + term
+        steep = a * (2 * 0.7978845608028654 + (6 * 0.044715 * 0.7978845608028654) * square)
+        slope = half + (half - half * half) * steep
+        d_inner.append((d_hidden[:, part] * slope).astype(BF16))
+    back = nn(jnp.concatenate(d_inner, axis=1), mlp_in_t[...])
     grad2 = gradient + norm_back(stream2, r3, back)
 
     back2 = nn(grad2.astype(BF16), axial_out_t[...]).astype(BF16)
@@ -366,11 +366,12 @@
 
     hidden_out = nn(jnp.concatenate(hidden, axis=1), mlp_out[...])
     lo_send[...] = (stream2 + hidden_out).astype(BF16).reshape(8, 16, C)
+    win_out_t[...] = win_out[...].T
+    win_kv_t[0:C] = win_qkv[:, 2 * C : 3 * C].T
+    win_kv_t[C : 2 * C] = win_qkv[:, C : 2 * C].T
+
+    grad1_bf = arrived(g1_send, g1_recv, 3)
     lo_copies = exchange(lo_send, lo_recv, 2)
-    win_out_t[...] = win_out[...].T
-    win_kv_t[...] = win_qkv[:, C : 3 * C].T
-
-    grad1_bf = arrived(g1_send, g1_recv, 3)
     back1 = nn(grad1_bf, win_out_t[...]).astype(BF16)
     back1_t = nt(win_out[...], grad1_bf).astype(BF16).astype(F32)
     upstream, delta = [], []
@@ -388,7 +389,7 @@
             d_scores.append((weights.astype(F32) * (d_weights - delta[p])).astype(BF16))
             d_key.append(nn(d_scores[p], q1[p]).astype(BF16))
             d_value.append(nn(weights, upstream[p]).astype(BF16))
-        d_kv = jnp.concatenate(d_key + d_value, axis=1)
+        d_kv = jnp.concatenate(d_value + d_key, axis=1)
         return d_scores, nn(d_kv, win_kv_t[...])
 
     push = []

time: 37.7 us -> 38.3 us (1.016)
  Pallas kernels: 36.9 us -> 37.6 us
    pallas_call x1, Pallas kernels: 36.2 us -> 36.8 us  [shards(): pl.pallas_call(functools.partial(kernel, nx, ny), out_shape=(pltpu.VMEM((...]
where the time goes in v6:
time: 38.3 us; the launch traced here: 38.2 us
  Pallas kernels  37.6 us (98%)
  between operations  0.64 us (2%)
    pallas_call x1, Pallas kernels, shards(): pl.pallas_call(functools.partial(kernel, nx, ny), out_shape=(pltpu.VMEM((...  36.8 us

profile of v6, /device:TPU:1, one launch (start us, length us, event | category | flops | bytes accessed | tf_op | source)
XLA Modules:
  0.0 38.2 jit_solution(7375692684058856528)
XLA Ops:
  0.6 36.8 %shard_map.104 = (bf16[128,384]{1,0:T(8,128)(2,1)S(1)}, f32[128,384]{1,0:T(8,128)S(1)}) custom-call(bf16[2,4,16,384]{3,2,1,0:T(8,128)(2,1)} %bitcast.5, bf16[8,16,384]{2,1,0:T(8,128)(2,1)} %bitcast.6, bf16[384,1152]{1,0:T(8,128)(2,1)} %win_qkv_h.1, bf16[384,384]{1,0:T(8,128)(2,1)} %win_out_h.1, bf16[384,1152]{1,0:T(8,128)(2,1)} %axial_qkv_h.1, ...), custom_call_target="tpu_custom_call" | custom-call | tf_op jit(solution)/shard_map/pallas_call | solution.py:472
  37.5 0.7 %shard_map.105 = (bf16[128,384]{1,0:T(8,128)(2,1)}, f32[128,384]{1,0:T(8,128)}) custom-call(bf16[128,384]{1,0:T(8,128)(2,1)S(1)} %get-tuple-element.6.out_ref, f32[128,384]{1,0:T(8,128)S(1)} %get-tuple-element.7.grad_ref), custom_call_target="tpu_custom_call" | custom-call | tf_op jit(solution)/shard_map/pallas_call | solution.py:505

commit v7 on v6

--- a/solution.py
+++ b/solution.py
@@ -164,9 +164,8 @@
             device_id=at(dx, dy),
             device_id_type=MESH,
         )
+        copy.start()
         halo.append(copy)
-    for copy in halo[:6]:
-        copy.start()
     for copy in local[2:]:
         copy.start()
 
@@ -228,9 +227,6 @@
         else:
             start = 384 + 32 * index
             bias1[start : start + 32, :] = near(32, 1, -2 * dx, -2 if dy == 1 else 8)
-
-    for copy in halo[6:]:
-        copy.start()
 
     def window_scores(part, tokens):
         values = tokens.astype(F32)

time: 38.3 us -> 38.3 us (level)
  no operation moved by 1% of the time
where the time goes in v7:
time: 38.3 us; the launch traced here: 38.2 us
  Pallas kernels  37.6 us (98%)
  between operations  0.64 us (2%)
    pallas_call x1, Pallas kernels, shards(): pl.pallas_call(functools.partial(kernel, nx, ny), out_shape=(pltpu.VMEM((...  36.8 us

profile of v7, /device:TPU:1, one launch (start us, length us, event | category | flops | bytes accessed | tf_op | source)
XLA Modules:
  0.0 38.2 jit_solution(3826770836555266233)
XLA Ops:
  0.6 36.8 %shard_map.104 = (bf16[128,384]{1,0:T(8,128)(2,1)S(1)}, f32[128,384]{1,0:T(8,128)S(1)}) custom-call(bf16[2,4,16,384]{3,2,1,0:T(8,128)(2,1)} %bitcast.5, bf16[8,16,384]{2,1,0:T(8,128)(2,1)} %bitcast.6, bf16[384,1152]{1,0:T(8,128)(2,1)} %win_qkv_h.1, bf16[384,384]{1,0:T(8,128)(2,1)} %win_out_h.1, bf16[384,1152]{1,0:T(8,128)(2,1)} %axial_qkv_h.1, ...), custom_call_target="tpu_custom_call" | custom-call | tf_op jit(solution)/shard_map/pallas_call | solution.py:468
  37.5 0.7 %shard_map.105 = (bf16[128,384]{1,0:T(8,128)(2,1)}, f32[128,384]{1,0:T(8,128)}) custom-call(bf16[128,384]{1,0:T(8,128)(2,1)S(1)} %get-tuple-element.6.out_ref, f32[128,384]{1,0:T(8,128)S(1)} %get-tuple-element.7.grad_ref), custom_call_target="tpu_custom_call" | custom-call | tf_op jit(solution)/shard_map/pallas_call | solution.py:501

commit v8 on v7

--- a/solution.py
+++ b/solution.py
@@ -362,12 +362,12 @@
 
     hidden_out = nn(jnp.concatenate(hidden, axis=1), mlp_out[...])
     lo_send[...] = (stream2 + hidden_out).astype(BF16).reshape(8, 16, C)
+    lo_copies = exchange(lo_send, lo_recv, 2)
     win_out_t[...] = win_out[...].T
     win_kv_t[0:C] = win_qkv[:, 2 * C : 3 * C].T
     win_kv_t[C : 2 * C] = win_qkv[:, C : 2 * C].T
 
     grad1_bf = arrived(g1_send, g1_recv, 3)
-    lo_copies = exchange(lo_send, lo_recv, 2)
     back1 = nn(grad1_bf, win_out_t[...]).astype(BF16)
     back1_t = nt(win_out[...], grad1_bf).astype(BF16).astype(F32)
     upstream, delta = [], []

time: 38.3 us -> 37.7 us (0.984)
  Pallas kernels: 37.6 us -> 37 us
    pallas_call x1, Pallas kernels: 36.8 us -> 36.3 us  [shards(): pl.pallas_call(functools.partial(kernel, nx, ny), out_shape=(pltpu.VMEM((...]
where the time goes in v8:
time: 37.7 us; the launch traced here: 37.6 us
  Pallas kernels  37 us (98%)
  between operations  0.64 us (2%)
    pallas_call x1, Pallas kernels, shards(): pl.pallas_call(functools.partial(kernel, nx, ny), out_shape=(pltpu.VMEM((...  36.3 us

profile of v8, /device:TPU:1, one launch (start us, length us, event | category | flops | bytes accessed | tf_op | source)
XLA Modules:
  0.0 37.6 jit_solution(13379727708036733361)
XLA Ops:
  0.6 36.3 %shard_map.104 = (bf16[128,384]{1,0:T(8,128)(2,1)S(1)}, f32[128,384]{1,0:T(8,128)S(1)}) custom-call(bf16[2,4,16,384]{3,2,1,0:T(8,128)(2,1)} %bitcast.5, bf16[8,16,384]{2,1,0:T(8,128)(2,1)} %bitcast.6, bf16[384,1152]{1,0:T(8,128)(2,1)} %win_qkv_h.1, bf16[384,384]{1,0:T(8,128)(2,1)} %win_out_h.1, bf16[384,1152]{1,0:T(8,128)(2,1)} %axial_qkv_h.1, ...), custom_call_target="tpu_custom_call" | custom-call | tf_op jit(solution)/shard_map/pallas_call | solution.py:468
  36.9 0.7 %shard_map.105 = (bf16[128,384]{1,0:T(8,128)(2,1)}, f32[128,384]{1,0:T(8,128)}) custom-call(bf16[128,384]{1,0:T(8,128)(2,1)S(1)} %get-tuple-element.6.out_ref, f32[128,384]{1,0:T(8,128)S(1)} %get-tuple-element.7.grad_ref), custom_call_target="tpu_custom_call" | custom-call | tf_op jit(solution)/shard_map/pallas_call | solution.py:501

commit v9 on v8

--- a/solution.py
+++ b/solution.py
@@ -103,6 +103,7 @@
     vt1,
     ot1,
     scores1,
+    edge_values,
     bias1,
     q1,
     local_sem,
@@ -363,6 +364,14 @@
     hidden_out = nn(jnp.concatenate(hidden, axis=1), mlp_out[...])
     lo_send[...] = (stream2 + hidden_out).astype(BF16).reshape(8, 16, C)
     lo_copies = exchange(lo_send, lo_recv, 2)
+    feature = iota((TOK, C), 0)
+    upper = jnp.where(feature < 64, 1.0, 0.0).astype(BF16)
+    lower = jnp.where(feature < 64, 0.0, 1.0).astype(BF16)
+    for p in range(PAIRS):
+        rows = win_out[lanes(p), :]
+        values = kv1[EDGES, lanes(p, C)]
+        edge_values[2 * p] = nn(values, rows * upper).astype(BF16)
+        edge_values[2 * p + 1] = nn(values, rows * lower).astype(BF16)
     win_out_t[...] = win_out[...].T
     win_kv_t[0:C] = win_qkv[:, 2 * C : 3 * C].T
     win_kv_t[C : 2 * C] = win_qkv[:, C : 2 * C].T
@@ -381,7 +390,11 @@
         d_scores, d_key, d_value = [], [], []
         for p in range(PAIRS):
             weights = weights1[p, part]
-            d_weights = nt(kv1[part, lanes(p, C)], upstream[p])
+            if part == EDGES:
+                halves = [nt(edge_values[2 * p + h], grad1_bf) for h in range(2)]
+                d_weights = jnp.concatenate(halves, axis=1)
+            else:
+                d_weights = nt(kv1[part, lanes(p, C)], upstream[p])
             d_scores.append((weights.astype(F32) * (d_weights - delta[p])).astype(BF16))
             d_key.append(nn(d_scores[p], q1[p]).astype(BF16))
             d_value.append(nn(weights, upstream[p]).astype(BF16))
@@ -484,6 +497,7 @@
             vmem((PAIRS, TOK, KEYS), BF16),
             vmem((PAIRS, TOK, TOK), F32),
             vmem((PAIRS, KEYS, 256), F32),
+            vmem((2 * PAIRS, 192, C), BF16),
             vmem((KEYS, TOK), F32),
             vmem((PAIRS, 256, TOK), BF16),
             dma((9,)),

time: 37.7 us -> 37.9 us (level)
  no operation moved by 1% of the time
where the time goes in v9:
time: 37.9 us; the launch traced here: 37.7 us
  Pallas kernels  37.1 us (98%)
  between operations  0.64 us (2%)
    pallas_call x1, Pallas kernels, shards(): pl.pallas_call(functools.partial(kernel, nx, ny), out_shape=(pltpu.VMEM((...  36.4 us

profile of v9, /device:TPU:1, one launch (start us, length us, event | category | flops | bytes accessed | tf_op | source)
XLA Modules:
  0.0 37.7 jit_solution(13546495149398115578)
XLA Ops:
  0.6 36.4 %shard_map.104 = (bf16[128,384]{1,0:T(8,128)(2,1)S(1)}, f32[128,384]{1,0:T(8,128)S(1)}) custom-call(bf16[2,4,16,384]{3,2,1,0:T(8,128)(2,1)} %bitcast.5, bf16[8,16,384]{2,1,0:T(8,128)(2,1)} %bitcast.6, bf16[384,1152]{1,0:T(8,128)(2,1)} %win_qkv_h.1, bf16[384,384]{1,0:T(8,128)(2,1)} %win_out_h.1, bf16[384,1152]{1,0:T(8,128)(2,1)} %axial_qkv_h.1, ...), custom_call_target="tpu_custom_call" | custom-call | tf_op jit(solution)/shard_map/pallas_call | solution.py:481
  37.0 0.7 %shard_map.105 = (bf16[128,384]{1,0:T(8,128)(2,1)}, f32[128,384]{1,0:T(8,128)}) custom-call(bf16[128,384]{1,0:T(8,128)(2,1)S(1)} %get-tuple-element.6.out_ref, f32[128,384]{1,0:T(8,128)S(1)} %get-tuple-element.7.grad_ref), custom_call_target="tpu_custom_call" | custom-call | tf_op jit(solution)/shard_map/pallas_call | solution.py:515

commit v10 on v8

--- a/solution.py
+++ b/solution.py
@@ -264,8 +264,8 @@
         outs.append(diagonal(nn(vt1[p, :, EARLY], e.astype(BF16))))
     for copy in halo[:6]:
         copy.wait_recv()
+    window_scores(EDGES, edges[...].reshape(192, C))
     cot_copies = exchange(cot_send, cot_recv, 0)
-    window_scores(EDGES, edges[...].reshape(192, C))
     attended, early_scale = [], []
     for p in range(PAIRS):
         scores = scores1[p, EDGES]
@@ -424,7 +424,9 @@
         d_query.append((diagonal(both) * 0.125).astype(BF16))
     d_query = nt(to_xyz, jnp.concatenate(d_query, axis=0)).astype(BF16)
     d_normed = d_normed + nt(d_query, win_qkv[:, 0:C])
-    grad1_xyz = nn(to_xyz, grad1_bf)
+    field_f = own[...].reshape(TOK, C).astype(F32)
+    r1 = inverse_rms(field_f)
+    grad_ref[...] = nn(to_xyz, grad1_bf)
     out_ref[...] = nn(to_xyz, arrived(lo_send, lo_recv, 2)).astype(BF16)
     for copy in push:
         copy.wait_recv()
@@ -439,8 +441,7 @@
     ]
     none = jnp.zeros((32, C), F32)
     rims = jnp.concatenate([first[0], none, last[0], first[1], none, last[1]], axis=0)
-    field_f = own[...].reshape(TOK, C).astype(F32)
-    grad_ref[...] = grad1_xyz + norm_back(field_f, inverse_rms(field_f), d_normed + rims)
+    grad_ref[...] += norm_back(field_f, r1, d_normed + rims)
 
     for copy in halo + cot_copies + s1_copies + lo_copies + g1_copies + push:
         copy.wait_send()

time: 37.7 us -> 37.8 us (level)
  no operation moved by 1% of the time
where the time goes in v10:
time: 37.8 us; the launch traced here: 37.7 us
  Pallas kernels  37 us (98%)
  between operations  0.64 us (2%)
    pallas_call x1, Pallas kernels, shards(): pl.pallas_call(functools.partial(kernel, nx, ny), out_shape=(pltpu.VMEM((...  36.3 us

profile of v10, /device:TPU:1, one launch (start us, length us, event | category | flops | bytes accessed | tf_op | source)
XLA Modules:
  0.0 37.7 jit_solution(5480318843178404335)
XLA Ops:
  0.6 36.3 %shard_map.104 = (bf16[128,384]{1,0:T(8,128)(2,1)S(1)}, f32[128,384]{1,0:T(8,128)S(1)}) custom-call(bf16[2,4,16,384]{3,2,1,0:T(8,128)(2,1)} %bitcast.5, bf16[8,16,384]{2,1,0:T(8,128)(2,1)} %bitcast.6, bf16[384,1152]{1,0:T(8,128)(2,1)} %win_qkv_h.1, bf16[384,384]{1,0:T(8,128)(2,1)} %win_out_h.1, bf16[384,1152]{1,0:T(8,128)(2,1)} %axial_qkv_h.1, ...), custom_call_target="tpu_custom_call" | custom-call | tf_op jit(solution)/shard_map/pallas_call | solution.py:469
  36.9 0.7 %shard_map.105 = (bf16[128,384]{1,0:T(8,128)(2,1)}, f32[128,384]{1,0:T(8,128)}) custom-call(bf16[128,384]{1,0:T(8,128)(2,1)S(1)} %get-tuple-element.6.out_ref, f32[128,384]{1,0:T(8,128)S(1)} %get-tuple-element.7.grad_ref), custom_call_target="tpu_custom_call" | custom-call | tf_op jit(solution)/shard_map/pallas_call | solution.py:502

commit v11 on v10

--- a/solution.py
+++ b/solution.py
@@ -264,8 +264,8 @@
         outs.append(diagonal(nn(vt1[p, :, EARLY], e.astype(BF16))))
     for copy in halo[:6]:
         copy.wait_recv()
+    cot_copies = exchange(cot_send, cot_recv, 0)
     window_scores(EDGES, edges[...].reshape(192, C))
-    cot_copies = exchange(cot_send, cot_recv, 0)
     attended, early_scale = [], []
     for p in range(PAIRS):
         scores = scores1[p, EDGES]

time: 37.8 us -> 37.7 us (level)
  no operation moved by 1% of the time
where the time goes in v11:
time: 37.7 us; the launch traced here: 37.6 us
  Pallas kernels  37 us (98%)
  between operations  0.64 us (2%)
    pallas_call x1, Pallas kernels, shards(): pl.pallas_call(functools.partial(kernel, nx, ny), out_shape=(pltpu.VMEM((...  36.2 us

profile of v11, /device:TPU:1, one launch (start us, length us, event | category | flops | bytes accessed | tf_op | source)
XLA Modules:
  0.0 37.6 jit_solution(5020222508800628153)
XLA Ops:
  0.6 36.2 %shard_map.104 = (bf16[128,384]{1,0:T(8,128)(2,1)S(1)}, f32[128,384]{1,0:T(8,128)S(1)}) custom-call(bf16[2,4,16,384]{3,2,1,0:T(8,128)(2,1)} %bitcast.5, bf16[8,16,384]{2,1,0:T(8,128)(2,1)} %bitcast.6, bf16[384,1152]{1,0:T(8,128)(2,1)} %win_qkv_h.1, bf16[384,384]{1,0:T(8,128)(2,1)} %win_out_h.1, bf16[384,1152]{1,0:T(8,128)(2,1)} %axial_qkv_h.1, ...), custom_call_target="tpu_custom_call" | custom-call | tf_op jit(solution)/shard_map/pallas_call | solution.py:469
  36.9 0.7 %shard_map.105 = (bf16[128,384]{1,0:T(8,128)(2,1)}, f32[128,384]{1,0:T(8,128)}) custom-call(bf16[128,384]{1,0:T(8,128)(2,1)S(1)} %get-tuple-element.6.out_ref, f32[128,384]{1,0:T(8,128)S(1)} %get-tuple-element.7.grad_ref), custom_call_target="tpu_custom_call" | custom-call | tf_op jit(solution)/shard_map/pallas_call | solution.py:502
